TPU v7x, 512 devices: a whole 4x4x16 slice. The times are simulated.
512 devices in a mesh: tile: 32 (over y, x, core), member: 16 (over z).
Axes of the slice: x: 4, y: 4, z: 16, core: 2. Of those that a mesh axis runs over, the one named last changes fastest.
Arguments:
- hx: bfloat16 [512, 131072], P('member', 'tile'), may hold values from -6 to 6
- obs_value: bfloat16 [131072], P('tile'), may hold values from -8 to 8
- obs_rinv: bfloat16 [131072], P('tile'), may hold values from 0.29882812 to 4
- obs_index: int32 [512, 1024], P('tile'), may hold values from 128 to 6015, as said below
- loc_weight: float32 [512, 1024], P(('tile', 'member')), may hold values from 0.05 to 1
- state: bfloat16 [512, 524288], P('member', 'tile'), may hold values from -6 to 6
Outputs:
- analysis: bfloat16 [512, 524288], P('member', 'tile')
Inputs may be any that keep to these rules, and one draw needn't show every extreme that they name: `obs_index`: row p lists 1024 distinct positions in the pool of tile p // 16: positions 0 .. 1023 are the last 1024 observations of the tile before it, the next 4096 the tile's own, the last 1024 the first observations of the tile after it; the tiles form a closed band. All positions of a row lie within 2048 consecutive positions.
All inputs are finite; a program needn't handle non-finite values.
Results may differ from a plain program's by a relative error of at most 0.012.
The roundings to bfloat16 on the way count: a program that leaves them out, or rounds other values in their place, can miss the bound.
Values may be sent and summed in bfloat16 or wider, within the bound.
A program may use at most 64 MiB of HBM per device.

v0:
```python
import jax
import jax.numpy as jnp
from jax import lax
from jax.sharding import PartitionSpec as P

LOC = 1024
NS_ITERS = 3


def with_halo(block, sides, width):
    for axis, dim in sides:
        count = lax.axis_size(axis)
        forward = [(i, i + 1) for i in range(count - 1)]
        forward.append((count - 1, 0))
        backward = [(target, source) for source, target in forward]
        low = lax.ppermute(
            lax.slice_in_dim(block, block.shape[dim] - width, None, axis=dim), axis, forward
        )
        high = lax.ppermute(lax.slice_in_dim(block, 0, width, axis=dim), axis, backward)
        block = jnp.concatenate([low, block, high], axis=dim)
    return block


def product_f32(left, right, dims):
    return lax.dot_general(
        left.astype(jnp.float32),
        right.astype(jnp.float32),
        (dims, ((), ())),
        precision=lax.Precision.HIGHEST,
        preferred_element_type=jnp.float32,
    )


def analysis(obs_block, obs_pair, loc_row):
    members = obs_block.shape[0]
    block_f = obs_block.astype(jnp.float32)
    obs_mean = jnp.mean(block_f, axis=0)
    obs_root = jnp.sqrt(obs_pair[1].astype(jnp.float32) * loc_row)
    scaled = ((block_f - obs_mean) * obs_root).astype(jnp.bfloat16)
    innovation = (obs_pair[0].astype(jnp.float32) - obs_mean) * obs_root
    gram_matrix = product_f32(scaled, scaled, ((1,), (1,)))
    identity = jnp.eye(members, dtype=jnp.float32)
    system = gram_matrix + (members - 1.0) * identity
    projection = jnp.dot(scaled.astype(jnp.float32), innovation, precision=lax.Precision.HIGHEST)
    norm_a = jnp.sqrt(jnp.sum(system * system))
    upper_iter = system / norm_a
    lower_iter = identity
    for sweep in range(NS_ITERS):
        upper_b = upper_iter.astype(jnp.bfloat16)
        lower_b = lower_iter.astype(jnp.bfloat16)
        product = product_f32(lower_b, upper_b, ((1,), (0,)))
        half_step = (1.5 * identity - 0.5 * product).astype(jnp.bfloat16)
        if sweep + 1 < NS_ITERS:
            upper_iter = product_f32(upper_b, half_step, ((1,), (0,)))
        lower_iter = product_f32(half_step, lower_b, ((1,), (0,)))
    invroot = lower_iter / jnp.sqrt(norm_a)
    inner_w = jnp.dot(invroot, projection, precision=lax.Precision.HIGHEST)
    mean_w = jnp.dot(invroot, inner_w, precision=lax.Precision.HIGHEST)
    transform = jnp.sqrt(members - 1.0) * invroot + mean_w[:, None]
    return transform.astype(jnp.bfloat16)


def transform_state(transform, state_block):
    block_f = state_block.astype(jnp.float32)
    state_mean = jnp.mean(block_f, axis=0)
    state_pert = (block_f - state_mean).astype(jnp.bfloat16)
    combined = product_f32(transform, state_pert, ((0,), (0,)))
    return (state_mean + combined).astype(jnp.bfloat16)


def on_device(hx, obs_value, obs_rinv, obs_index, loc_weight, state):
    ens_dev = hx.shape[0]
    member_pos = lax.axis_index("member")
    stacked = jnp.concatenate([hx, obs_value[None, :], obs_rinv[None, :]], axis=0)
    obs_pool = with_halo(stacked, (("tile", 1),), LOC)
    own_index = lax.dynamic_index_in_dim(obs_index, member_pos, 0, keepdims=False)
    obs_pair = jnp.take(obs_pool[ens_dev:], own_index, axis=1)
    all_rows = lax.all_gather(obs_pool[:ens_dev], "member", axis=0, tiled=True)
    obs_block = jnp.take(all_rows, own_index, axis=1)
    transform = analysis(obs_block, obs_pair, loc_weight[0])
    group_count = obs_index.shape[0]
    state_split = state.reshape(ens_dev, group_count, state.shape[1] // group_count)
    updated = transform_state(
        transform,
        lax.all_to_all(state_split, "member", split_axis=1, concat_axis=0, tiled=True)[:, 0, :],
    )
    result = lax.all_to_all(updated[:, None, :], "member", split_axis=0, concat_axis=1, tiled=True)
    return result.reshape(ens_dev, state.shape[1])


def solution(mesh):
    in_specs = (
        P("member", "tile"),
        P("tile"),
        P("tile"),
        P("tile", None),
        P(("tile", "member"), None),
        P("member", "tile"),
    )
    out_specs = P("member", "tile")
    return jax.shard_map(
        on_device, mesh=mesh, in_specs=in_specs, out_specs=out_specs, check_vma=False
    )
```

profile of v0, /device:TPU:16, one launch (start us, length us, event | category | flops | bytes accessed | tf_op | source)
XLA Modules:
  0.0 249.0 jit_solution(11522932096585671620)
XLA Ops:
  6.5 0.0 copy-start.1
  6.5 0.0 all-gather.2.cloned.1.call-start
  6.5 0.8 broadcast_in_dim.35
  7.3 0.7 broadcast_in_dim.36
  8.1 0.9 pad_maximum_fusion.3
  9.0 1.9 collective-permute-start
  10.9 5.8 %collective-permute-start.1 = (bf16[34,1024]{1,0:T(8,128)(2,1)S(1)}, bf16[34,1024]{1,0:T(8,128)(2,1)S(1)}, u32[]{:S(2)}, u32[]{:S(2)}) collective-permute-start(bf16[34,1024]{1,0:T(8,128)(2,1)S(1)} %get-tuple-element.8), channel_id=1, source_target_pairs={{16,0},{32,16},{48,32},{64,48},{80,64},{96,80},{112,96},{128,112},... | collective-permute-start | bytes 208904 | tf_op jit(solution)/shard_map/ppermute | solution.py:19
  16.6 0.2 collective-permute-done
  16.8 1.9 collective-permute-done.1
  18.7 1.0 pad_maximum_fusion
  19.7 0.8 slice.28
  20.5 0.0 all-gather.2.cloned.1.call-update
  20.5 0.0 copy-done.1
  20.5 0.0 copy-start
  20.5 1.1 copy.44
  21.6 15.2 %all-to-all-start = ((bf16[32,16,1024]{2,0,1:T(8,128)(2,1)}), bf16[32,16,1024]{2,0,1:T(8,128)(2,1)S(1)}, u32[]{:S(2)}, u32[]{:S(2)}) async-start(bf16[32,16,1024]{2,0,1:T(8,128)(2,1)} %bitcast.59), calls=%async_computation | async-start | bytes 2097152 | tf_op jit(solution)/shard_map/all_to_all | solution.py:85
  36.8 0.0 copy-start.2
  36.8 0.8 compare_select_fusion
  37.6 0.0 copy-done
  37.7 0.9 copy.34
  38.6 3.2 %gather_fusion.1 = bf16[1024,2]{1,0:T(8,128)(2,1)S(1)} fusion(bf16[2,6144]{0,1:T(8,128)(2,1)S(1)} %copy.34, s32[1024]{0:T(1024)S(1)} %broadcast_clamp_fusion), kind=kCustom, calls=%fused_computation.1 | custom fusion | bytes 12288 | tf_op jit(solution)/shard_map/jit(_take)/gather | solution.py:77
  41.8 0.2 select_bitcast_fusion
  42.0 0.1 slice.29
  42.1 0.1 copy.35
  42.3 0.0 copy-done.2
  42.3 0.2 copy.36
  42.5 0.1 convert_reduce_fusion.1
  42.7 0.2 sqrt_reduce_fusion
  42.9 53.0 %all-to-all-done = bf16[32,16,1024]{2,0,1:T(8,128)(2,1)S(1)} async-done(((bf16[32,16,1024]{2,0,1:T(8,128)(2,1)}), bf16[32,16,1024]{2,0,1:T(8,128)(2,1)S(1)}, u32[]{:S(2)}, u32[]{:S(2)}) %all-to-all-start) | async-done | bytes 1048608 | tf_op jit(solution)/shard_map/all_to_all | solution.py:85
  95.9 0.2 convert_reduce_fusion.2
  96.1 0.2 fusion.2
  96.4 54.4 %all-gather.2.cloned.1.call-done = bf16[512,6144]{1,0:T(8,128)(2,1)} async-done(((bf16[32,6144]{1,0:T(8,128)(2,1)}), bf16[512,6144]{1,0:T(8,128)(2,1)}) %all-gather.2.cloned.1.call-update) | async-done | bytes 6291472 | tf_op jit(solution)/shard_map/all_gather | solution.py:78
  150.8 8.6 %copy.33 = bf16[512,6144]{0,1:T(8,128)(2,1)} copy(bf16[512,6144]{1,0:T(8,128)(2,1)} %all-gather.2.cloned.1.call-done) | data formatting | bytes 12582912 | tf_op jit(solution)/shard_map/all_gather | solution.py:78
  159.4 7.6 %gather_fusion = bf16[1024,512]{1,0:T(8,128)(2,1)S(1)} fusion(bf16[512,6144]{0,1:T(8,128)(2,1)} %copy.33, s32[1024]{0:T(1024)S(1)} %broadcast_clamp_fusion), kind=kCustom, calls=%fused_computation | custom fusion | bytes 2101248 | tf_op jit(solution)/shard_map/jit(_take)/gather | solution.py:79
  167.0 0.5 convert_reduce_fusion
  167.5 0.9 fusion.1
  168.4 1.5 multiply_reduce_fusion
  170.7 0.4 fusion.4
  171.1 0.4 convolution_convert_fusion.2
  171.5 0.4 convolution_convert_fusion.3
  172.0 0.4 fusion.5
  172.4 0.4 convolution_convert_fusion.1
  172.9 0.4 convolution_convert_fusion
  173.3 0.5 convolution_bitcast_fusion.1
  173.8 0.5 fusion.6
  174.3 0.4 convolution_divide_fusion
  174.7 1.0 convolution_bitcast_fusion
  175.7 1.0 fusion.11
  176.7 0.8 fusion.3
  177.5 0.5 broadcast.96
  178.1 1.4 reduce.8
  179.5 0.8 reshape.88
  180.3 59.4 %all_to_all.24 = bf16[16,2,16384]{2,1,0:T(2,128)(2,1)S(1)} all-to-all(bf16[16,2,16384]{2,1,0:T(2,128)(2,1)S(1)} %reshape.88), channel_id=1, replica_groups=mesh['tile'=32,'member'=16] {'member'}, dimensions={0} | all-to-all | bytes 2097152 | tf_op jit(solution)/shard_map/all_to_all | solution.py:87
  239.7 1.0 reshape.89
  240.7 0.4 copy.39
  241.1 1.1 copy.41
  (6 shorter events, 0.1 us)
Async XLA Ops:
  6.5 14.0 %copy-start.1 = (bf16[32,16384]{1,0:T(8,128)(2,1)S(1)}, bf16[32,16384]{1,0:T(8,128)(2,1)}, u32[]{:S(2)}) copy-start(bf16[32,16384]{1,0:T(8,128)(2,1)} %param.11) | copy-start | bytes 3145732
  6.5 144.3 %all-gather.2.cloned.1.call-start = ((), (), s32[]{:S(2)}) async-start(), calls=%async_computation.2 | async-start | bytes 6684672 | tf_op jit(solution)/shard_map/all_gather | solution.py:78
  9.0 7.9 %collective-permute-start = (bf16[34,1024]{1,0:T(8,128)(2,1)S(1)}, bf16[34,1024]{1,0:T(8,128)(2,1)S(1)}, u32[]{:S(2)}, u32[]{:S(2)}) collective-permute-start(bf16[34,1024]{1,0:T(8,128)(2,1)S(1)} %get-tuple-element.7), channel_id=1, source_target_pairs={{0,16},{16,32},{32,48},{48,64},{64,80},{80,96},{96,112},{112,128},... | collective-permute-start | bytes 208904 | tf_op jit(solution)/shard_map/ppermute | solution.py:16
  10.9 7.8 %collective-permute-start.1 = (bf16[34,1024]{1,0:T(8,128)(2,1)S(1)}, bf16[34,1024]{1,0:T(8,128)(2,1)S(1)}, u32[]{:S(2)}, u32[]{:S(2)}) collective-permute-start(bf16[34,1024]{1,0:T(8,128)(2,1)S(1)} %get-tuple-element.8), channel_id=1, source_target_pairs={{16,0},{32,16},{48,32},{64,48},{80,64},{96,80},{112,96},{128,112},... | collective-permute-start | bytes 208904 | tf_op jit(solution)/shard_map/ppermute | solution.py:19
  20.5 17.1 %copy-start = (bf16[32,4096]{1,0:T(8,128)(2,1)S(1)}, bf16[32,4096]{1,0:T(8,128)(2,1)}, u32[]{:S(2)}) copy-start(bf16[32,4096]{1,0:T(8,128)(2,1)} %param.6) | copy-start | bytes 786436
  21.6 74.3 %all-to-all-start = ((bf16[32,16,1024]{2,0,1:T(8,128)(2,1)}), bf16[32,16,1024]{2,0,1:T(8,128)(2,1)S(1)}, u32[]{:S(2)}, u32[]{:S(2)}) async-start(bf16[32,16,1024]{2,0,1:T(8,128)(2,1)} %bitcast.59), calls=%async_computation | async-start | bytes 2097152 | tf_op jit(solution)/shard_map/all_to_all | solution.py:85
  36.8 5.5 %copy-start.2 = (f32[1,1024]{1,0:T(1,128)S(1)}, f32[1,1024]{1,0:T(1,128)}, u32[]{:S(2)}) copy-start(f32[1,1024]{1,0:T(1,128)} %param.10) | copy-start | bytes 12292
Sparse Core Ops, SparseCore 0:
  20.6 130.1 all-gather.1
where the time goes:
time: 250 us; the launch traced here: 249 us
  waiting for transfers between devices  110 us (44%)
  blocking collectives  59.4 us (24%)
  local copies, waits for them, and re-layouts  28.2 us (11%)
  starting transfers between devices  22.9 us (9%)
  between operations  14.4 us (6%)
  matrix products  8.3 us (3%)
  other arithmetic  6.37 us (3%)
    all_to_all x1, blocking collectives, on_device(): lax.all_to_all(updated[:, None, :], 'member', split_axis=0, concat_axis=1...  59.4 us
    all_gather x1, waiting for transfers between devices, on_device(): all_rows = lax.all_gather(obs_pool[:ens_dev], 'member', axis=0, tiled=True)  54.4 us
    all_to_all x1, waiting for transfers between devices, on_device(): lax.all_to_all(state_split, 'member', split_axis=1, concat_axis=0, tiled=...  53 us
    all_to_all x1, starting transfers between devices, on_device(): lax.all_to_all(state_split, 'member', split_axis=1, concat_axis=0, tiled=...  15.2 us
    all_gather x1, local copies, waits for them, and re-layouts, on_device(): all_rows = lax.all_gather(obs_pool[:ens_dev], 'member', axis=0, tiled=True)  8.64 us
    gather x1, local copies, waits for them, and re-layouts, on_device(): obs_block = jnp.take(all_rows, own_index, axis=1)  7.58 us
    dot_general x10, matrix products, product_f32(): lax.dot_general(left.astype(jnp.float32), right.astype(jnp.float32), (dim...  5.82 us
    ppermute x1, starting transfers between devices, with_halo(): lax.ppermute(lax.slice_in_dim(block, 0, width, axis=dim), axis, backward)  5.75 us
  transfers between devices with their start and end apart: 4, of which 4 were waited for; matrix products, arithmetic and copies ran while one was open for 3% of the time, Pallas kernels for 0%

commit v1 on v0

--- a/solution.py
+++ b/solution.py
@@ -75,7 +75,10 @@
     obs_pool = with_halo(stacked, (("tile", 1),), LOC)
     own_index = lax.dynamic_index_in_dim(obs_index, member_pos, 0, keepdims=False)
     obs_pair = jnp.take(obs_pool[ens_dev:], own_index, axis=1)
-    all_rows = lax.all_gather(obs_pool[:ens_dev], "member", axis=0, tiled=True)
+    all_rows = jnp.concatenate(
+        lax.all_to_all(jnp.stack([obs_pool[:ens_dev]] * lax.axis_size("member")), "member", 0, 0),
+        axis=0,
+    )
     obs_block = jnp.take(all_rows, own_index, axis=1)
     transform = analysis(obs_block, obs_pair, loc_weight[0])
     group_count = obs_index.shape[0]

time: 250 us -> 450 us (1.80)
  waiting for transfers between devices: 110 us -> 308 us
  between operations: 14.4 us -> 1.1 us
  starting transfers between devices: 22.9 us -> 30.8 us
    all_to_all x0 -> x1, waiting for transfers between devices: none -> 266 us  [on_device(): lax.all_to_all(jnp.stack([obs_pool[:ens_dev]] * lax.axis_size('member')),...]
    all_gather x1 -> x0, waiting for transfers between devices: 54.4 us -> none  [on_device(): all_rows = lax.all_gather(obs_pool[:ens_dev], 'member', axis=0, tiled=True)]
    all_to_all x1, waiting for transfers between devices: 53 us -> 40.1 us  [on_device(): lax.all_to_all(state_split, 'member', split_axis=1, concat_axis=0, tiled=...]
    reshape x0 -> x1, local copies, waits for them, and re-layouts: none -> 8.64 us  [on_device(): jnp.concatenate(lax.all_to_all(jnp.stack([obs_pool[:ens_dev]] * lax.axis_...]
    all_gather x1 -> x0, local copies, waits for them, and re-layouts: 8.64 us -> none  [on_device(): all_rows = lax.all_gather(obs_pool[:ens_dev], 'member', axis=0, tiled=True)]
    all_to_all x0 -> x1, starting transfers between devices: none -> 7.92 us  [on_device(): lax.all_to_all(jnp.stack([obs_pool[:ens_dev]] * lax.axis_size('member')),...]
  transfers between devices with their start and end apart: 4 -> 4, of which waited for: 4 -> 4; matrix products, arithmetic and copies ran while one was open for 3% -> 1% of each run, Pallas kernels for 0% -> 0%
where the time goes in v1:
time: 450 us; the launch traced here: 449 us
  waiting for transfers between devices  308 us (68%)
  blocking collectives  62.2 us (14%)
  starting transfers between devices  30.8 us (7%)
  local copies, waits for them, and re-layouts  30.4 us (7%)
  matrix products  11.7 us (3%)
  other arithmetic  4.71 us (1%)
    all_to_all x1, waiting for transfers between devices, on_device(): lax.all_to_all(jnp.stack([obs_pool[:ens_dev]] * lax.axis_size('member')),...  266 us
    all_to_all x1, blocking collectives, on_device(): lax.all_to_all(updated[:, None, :], 'member', split_axis=0, concat_axis=1...  62.2 us
    all_to_all x1, waiting for transfers between devices, on_device(): lax.all_to_all(state_split, 'member', split_axis=1, concat_axis=0, tiled=...  40.1 us
    all_to_all x1, starting transfers between devices, on_device(): lax.all_to_all(state_split, 'member', split_axis=1, concat_axis=0, tiled=...  15.2 us
    dot_general x10, matrix products, product_f32(): lax.dot_general(left.astype(jnp.float32), right.astype(jnp.float32), (dim...  9.17 us
  transfers between devices with their start and end apart: 4, of which 4 were waited for; matrix products, arithmetic and copies ran while one was open for 1% of the time, Pallas kernels for 0%

profile of v1, /device:TPU:16, one launch (start us, length us, event | category | flops | bytes accessed | tf_op | source)
XLA Modules:
  0.0 448.8 jit_solution(3487662305579844857)
XLA Ops:
  0.0 0.0 copy-start.1
  0.0 0.0 copy-start.2
  0.0 0.0 copy-start
  0.0 2.3 copy.46
  2.3 15.2 %all-to-all-start = ((bf16[32,16,1024]{2,0,1:T(8,128)(2,1)}), bf16[32,16,1024]{2,0,1:T(8,128)(2,1)S(1)}, u32[]{:S(2)}, u32[]{:S(2)}) async-start(bf16[32,16,1024]{2,0,1:T(8,128)(2,1)} %bitcast.60), calls=%async_computation | async-start | bytes 2097152 | tf_op jit(solution)/shard_map/all_to_all | solution.py:88
  17.5 0.0 copy-done.1
  17.6 0.0 copy-done.2
  17.6 0.0 copy-done
  17.6 1.9 collective-permute-start
  19.6 5.8 %collective-permute-start.1 = (bf16[34,1024]{1,0:T(8,128)(2,1)S(1)}, bf16[34,1024]{1,0:T(8,128)(2,1)S(1)}, u32[]{:S(2)}, u32[]{:S(2)}) collective-permute-start(bf16[34,1024]{1,0:T(8,128)(2,1)S(1)} %get-tuple-element.8), channel_id=1, source_target_pairs={{16,0},{32,16},{48,32},{64,48},{80,64},{96,80},{112,96},{128,112},... | collective-permute-start | bytes 208904 | tf_op jit(solution)/shard_map/ppermute | solution.py:19
  25.3 0.2 collective-permute-done
  25.5 1.9 collective-permute-done.1
  27.4 0.1 pad_maximum_fusion
  27.5 40.1 %all-to-all-done = bf16[32,16,1024]{2,0,1:T(8,128)(2,1)S(1)} async-done(((bf16[32,16,1024]{2,0,1:T(8,128)(2,1)}), bf16[32,16,1024]{2,0,1:T(8,128)(2,1)S(1)}, u32[]{:S(2)}, u32[]{:S(2)}) %all-to-all-start) | async-done | bytes 1048608 | tf_op jit(solution)/shard_map/all_to_all | solution.py:88
  67.5 3.4 stack.2
  70.9 7.9 %all-to-all-start.1 = ((bf16[16,32,6144]{2,1,0:T(8,128)(2,1)}), bf16[16,32,6144]{2,1,0:T(8,128)(2,1)}, u32[]{:S(2)}, u32[]{:S(2)}) async-start(bf16[16,32,6144]{2,1,0:T(8,128)(2,1)} %stack.2), calls=%async_computation.1 | async-start | bytes 12582912 | tf_op jit(solution)/shard_map/all_to_all | solution.py:79
  78.9 0.0 copy-start.3
  78.9 0.8 compare_select_fusion
  79.7 0.9 copy.36
  80.6 3.2 gather_fusion.1
  83.8 0.2 select_bitcast_fusion
  84.1 0.1 slice.29
  84.2 0.1 copy.37
  84.3 0.0 copy-done.3
  84.4 0.2 copy.38
  84.6 0.3 convert_reduce_fusion.1
  84.9 0.2 convert_reduce_fusion.2
  85.1 0.2 fusion.2
  85.3 265.9 %all-to-all-done.1 = bf16[16,32,6144]{2,1,0:T(8,128)(2,1)} async-done(((bf16[16,32,6144]{2,1,0:T(8,128)(2,1)}), bf16[16,32,6144]{2,1,0:T(8,128)(2,1)}, u32[]{:S(2)}, u32[]{:S(2)}) %all-to-all-start.1) | async-done | bytes 6291488 | tf_op jit(solution)/shard_map/all_to_all | solution.py:79
  351.2 8.6 %copy.35 = bf16[512,6144]{0,1:T(8,128)(2,1)} copy(bf16[512,6144]{1,0:T(8,128)(2,1)} %bitcast.1) | data formatting | bytes 12582912 | tf_op jit(solution)/shard_map/reshape | solution.py:78
  359.9 7.6 %gather_fusion = bf16[1024,512]{1,0:T(8,128)(2,1)S(1)} fusion(bf16[512,6144]{0,1:T(8,128)(2,1)} %copy.35, s32[1024]{0:T(1024)S(1)} %broadcast_clamp_fusion), kind=kCustom, calls=%fused_computation | custom fusion | bytes 2101248 | tf_op jit(solution)/shard_map/jit(_take)/gather | solution.py:82
  367.5 0.5 convert_reduce_fusion
  368.0 0.9 fusion.1
  368.9 2.4 multiply_reduce_fusion
  372.0 1.7 fusion.4
  373.7 1.7 convolution_convert_fusion.2
  375.3 0.4 convolution_convert_fusion.3
  375.8 0.4 fusion.5
  376.2 0.4 convolution_convert_fusion
  376.6 0.4 convolution_convert_fusion.1
  377.1 0.5 convolution_bitcast_fusion.1
  377.6 0.5 fusion.6
  378.1 0.4 convolution_divide_fusion
  378.5 1.0 convolution_bitcast_fusion
  379.5 1.0 fusion.11
  380.5 0.8 fusion.3
  381.4 0.5 broadcast.98
  381.9 1.4 reduce.8
  383.3 0.8 reshape.94
  384.1 62.2 %all_to_all.29 = bf16[16,2,16384]{2,1,0:T(2,128)(2,1)S(1)} all-to-all(bf16[16,2,16384]{2,1,0:T(2,128)(2,1)S(1)} %reshape.94), channel_id=1, replica_groups=mesh['tile'=32,'member'=16] {'member'}, dimensions={0} | all-to-all | bytes 2097152 | tf_op jit(solution)/shard_map/all_to_all | solution.py:90
  446.3 1.0 reshape.95
  447.4 0.4 copy.41
  447.8 1.1 copy.43
  (10 shorter events, 0.2 us)
Async XLA Ops:
  0.0 17.5 %copy-start.1 = (bf16[4096]{0:T(1024)(128)(2,1)S(1)}, bf16[4096]{0:T(1024)(128)(2,1)}, u32[]{:S(2)}) copy-start(bf16[4096]{0:T(1024)(128)(2,1)} %param.7) | copy-start | bytes 24580
  0.0 17.6 %copy-start.2 = (bf16[4096]{0:T(1024)(128)(2,1)S(1)}, bf16[4096]{0:T(1024)(128)(2,1)}, u32[]{:S(2)}) copy-start(bf16[4096]{0:T(1024)(128)(2,1)} %param.8) | copy-start | bytes 24580
  0.0 17.6 %copy-start = (bf16[32,4096]{1,0:T(8,128)(2,1)S(1)}, bf16[32,4096]{1,0:T(8,128)(2,1)}, u32[]{:S(2)}) copy-start(bf16[32,4096]{1,0:T(8,128)(2,1)} %param.6) | copy-start | bytes 786436
  2.3 65.2 %all-to-all-start = ((bf16[32,16,1024]{2,0,1:T(8,128)(2,1)}), bf16[32,16,1024]{2,0,1:T(8,128)(2,1)S(1)}, u32[]{:S(2)}, u32[]{:S(2)}) async-start(bf16[32,16,1024]{2,0,1:T(8,128)(2,1)} %bitcast.60), calls=%async_computation | async-start | bytes 2097152 | tf_op jit(solution)/shard_map/all_to_all | solution.py:88
  17.6 7.9 %collective-permute-start = (bf16[34,1024]{1,0:T(8,128)(2,1)S(1)}, bf16[34,1024]{1,0:T(8,128)(2,1)S(1)}, u32[]{:S(2)}, u32[]{:S(2)}) collective-permute-start(bf16[34,1024]{1,0:T(8,128)(2,1)S(1)} %get-tuple-element.7), channel_id=1, source_target_pairs={{0,16},{16,32},{32,48},{48,64},{64,80},{80,96},{96,112},{112,128},... | collective-permute-start | bytes 208904 | tf_op jit(solution)/shard_map/ppermute | solution.py:16
  19.6 7.8 %collective-permute-start.1 = (bf16[34,1024]{1,0:T(8,128)(2,1)S(1)}, bf16[34,1024]{1,0:T(8,128)(2,1)S(1)}, u32[]{:S(2)}, u32[]{:S(2)}) collective-permute-start(bf16[34,1024]{1,0:T(8,128)(2,1)S(1)} %get-tuple-element.8), channel_id=1, source_target_pairs={{16,0},{32,16},{48,32},{64,48},{80,64},{96,80},{112,96},{128,112},... | collective-permute-start | bytes 208904 | tf_op jit(solution)/shard_map/ppermute | solution.py:19
  70.9 280.3 %all-to-all-start.1 = ((bf16[16,32,6144]{2,1,0:T(8,128)(2,1)}), bf16[16,32,6144]{2,1,0:T(8,128)(2,1)}, u32[]{:S(2)}, u32[]{:S(2)}) async-start(bf16[16,32,6144]{2,1,0:T(8,128)(2,1)} %stack.2), calls=%async_computation.1 | async-start | bytes 12582912 | tf_op jit(solution)/shard_map/all_to_all | solution.py:79
  78.9 5.5 %copy-start.3 = (f32[1,1024]{1,0:T(1,128)S(1)}, f32[1,1024]{1,0:T(1,128)}, u32[]{:S(2)}) copy-start(f32[1,1024]{1,0:T(1,128)} %param.10) | copy-start | bytes 12292
